TPU v7x, 512 devices: a whole 4x8x8 slice. The times are simulated.
512 devices in a mesh: ctx: 64 (over z, x, core), tp: 8 (over y).
Axes of the slice: x: 4, y: 8, z: 8, core: 2. Of those that a mesh axis runs over, the one named last changes fastest.
Arguments:
- queries: bfloat16 [8192, 64, 576], P('ctx', 'tp'), may hold values from -96 to 96
- latent_cache: bfloat16 [16, 8192, 576], P(None, ('ctx', 'tp')), may hold values from -16 to 16
- key_segments: int32 [1024, 128], replicated, may hold values from 0 to 2, as said below
- block_lists: int32 [64, 16], P('ctx'), may hold values from 0 to 1023, as said below
- value_up: bfloat16 [64, 512, 128], P('tp'), may hold values from -1 to 1
Outputs:
- attended: bfloat16 [8192, 8192], P('ctx', 'tp')
Inputs may be any that keep to these rules, and one draw needn't show every extreme that they name: `block_lists`: row b lists 16 different blocks; its first entry is (15) * 64 + b, the block of query block b itself, and the others lie before it. No two entries of a row are equal modulo 64. Every listed block holds some token of the query block's rollout. `key_segments`: rollout numbers never fall along the context; all query tokens lie in the last rollout.
All inputs are finite; a program needn't handle non-finite values.
Results may differ from a plain program's by a relative error of at most 0.014.
Values may be sent and summed in bfloat16 or wider, within the bound.
A program may use at most 64 MiB of HBM per device.

v0:
```python
import jax
import jax.numpy as jnp
from jax import lax
from jax.sharding import PartitionSpec as P

DC = 512
DR = 64
DN = 128


def shards(queries, latent_cache, key_segments, block_lists, value_up):
    owners = lax.axis_size("ctx")
    own_index = lax.axis_index("ctx")
    depth = latent_cache.shape[0]
    requests = lax.all_gather(block_lists, "ctx", axis=0, tiled=True)
    matched = requests % owners == own_index
    level_hit = jnp.sum(jnp.where(matched, requests // owners, 0), axis=1)
    chooser = (
        (level_hit[:, None] == jnp.arange(depth, dtype=jnp.int32)[None, :])
        & jnp.any(matched, axis=1)[:, None]
    ).astype(jnp.bfloat16)
    wanted = block_lists[0]
    picker = ((wanted % owners)[:, None] == jnp.arange(owners, dtype=jnp.int32)[None, :]).astype(
        jnp.bfloat16
    )
    whole = lax.all_gather(latent_cache, "tp", axis=1, tiled=True)
    outgoing = jnp.einsum("nk,krd->nrd", chooser, whole, preferred_element_type=jnp.float32).astype(
        jnp.bfloat16
    )
    incoming = lax.all_to_all(outgoing, "ctx", split_axis=0, concat_axis=0, tiled=True)
    blocks = jnp.einsum("tn,nrd->trd", picker, incoming, preferred_element_type=jnp.float32).astype(
        jnp.bfloat16
    )
    block_len = blocks.shape[1]
    key_rows = blocks.reshape(-1, blocks.shape[2])
    token_index = jnp.arange(block_len, dtype=jnp.int32)
    key_pos = (wanted[:, None] * block_len + token_index[None, :]).reshape(-1)
    key_seg = key_segments[wanted].reshape(-1)
    own_block = (depth - 1) * owners + own_index
    query_pos = own_block * block_len + token_index
    query_seg = lax.dynamic_index_in_dim(key_segments, own_block, 0, keepdims=False)
    allowed = (key_pos[None, :] <= query_pos[:, None]) & (key_seg[None, :] == query_seg[:, None])
    scale = (DN + DR) ** (-0.5)
    scores = (
        jnp.einsum("qhd,kd->qhk", queries, key_rows, preferred_element_type=jnp.float32) * scale
    )
    row_max = jnp.max(jnp.where(allowed[:, None, :], scores, -jnp.inf), axis=2, keepdims=True)
    weights = jnp.where(allowed[:, None, :], jnp.exp(scores - row_max), 0.0)
    probs = (weights / jnp.sum(weights, axis=2, keepdims=True)).astype(jnp.bfloat16)
    latent_out = jnp.einsum(
        "qhk,kc->qhc", probs, key_rows[:, :DC], preferred_element_type=jnp.float32
    ).astype(jnp.bfloat16)
    values = jnp.einsum(
        "qhc,hcv->qhv", latent_out, value_up, preferred_element_type=jnp.float32
    ).astype(jnp.bfloat16)
    return values.reshape(values.shape[0], -1)


def solution(mesh):
    return jax.shard_map(
        shards,
        mesh=mesh,
        in_specs=(
            P("ctx", "tp", None),
            P(None, ("ctx", "tp"), None),
            P(),
            P("ctx", None),
            P("tp", None, None),
        ),
        out_specs=P("ctx", "tp"),
        check_vma=False,
    )
```

profile of v0, /device:TPU:2, one launch (start us, length us, event | category | flops | bytes accessed | tf_op | source)
XLA Modules:
  0.0 345.2 jit_solution(16880746746276386248)
XLA Ops:
  6.5 0.0 copy-start
  6.5 0.0 all-gather.3.cloned.1.call-start
  6.5 0.7 all-gather.3.cloned.1.call-update
  7.3 44.7 %all-gather = s32[64,1,16]{2,1,0:T(1,128)S(1)} all-gather(s32[1,1,16]{2,1,0:T(1,128)} %bitcast.66), channel_id=1, replica_groups=mesh['ctx'=64,'tp'=8] {'ctx'}, dimensions={0}, use_global_device_ids=true | all-gather | bytes 4160 | tf_op jit(solution)/shard_map/all_gather | solution.py:15
  52.0 0.1 fusion.35
  52.1 0.1 fusion.19
  52.2 6.7 %all-gather.3.cloned.1.call-done = bf16[16,128,576]{2,1,0:T(8,128)(2,1)} async-done(((bf16[16,16,576]{2,1,0:T(8,128)(2,1)}), bf16[16,128,576]{2,1,0:T(8,128)(2,1)}) %all-gather.3.cloned.1.call-update) | async-done | bytes 2359312 | tf_op jit(solution)/shard_map/all_gather | solution.py:26
  58.9 4.0 %copy.11 = bf16[16,128,576]{1,0,2:T(8,128)(2,1)S(1)} copy(bf16[16,128,576]{2,1,0:T(8,128)(2,1)} %all-gather.3.cloned.1.call-done) | data formatting | bytes 4718592 | tf_op jit(solution)/shard_map/all_gather | solution.py:26
  63.0 5.1 %fusion.23 = bf16[64,128,576]{1,0,2:T(8,128)(2,1)} fusion(bf16[16,128,576]{1,0,2:T(8,128)(2,1)S(1)} %copy.11, s32[64]{0:T(128)S(1)} %fusion.19, pred[64]{0:T(512)(128)(4,1)S(1)} %get-tuple-element.5), kind=kOutput, calls=%fused_computation.36 | convolution fusion | flops 150996992 | bytes 11796800 | tf_op jit(solution)/shard_map/nk,krd->nrd/dot_general | solution.py:27
  68.1 13.4 %copy.21 = bf16[64,128,576]{1,2,0:T(8,128)(2,1)} copy(bf16[64,128,576]{1,0,2:T(8,128)(2,1)} %fusion.23) | data formatting | bytes 18874368 | tf_op jit(solution)/shard_map/nk,krd->nrd/dot_general | solution.py:27
  81.4 11.4 %all-to-all-start = ((bf16[64,128,576]{1,2,0:T(8,128)(2,1)}), bf16[64,128,576]{1,2,0:T(8,128)(2,1)}, u32[]{:S(2)}, u32[]{:S(2)}) async-start(bf16[64,128,576]{1,2,0:T(8,128)(2,1)} %copy.21), calls=%async_computation | async-start | bytes 18874368 | tf_op jit(solution)/shard_map/all_to_all | solution.py:30
  92.8 0.0 copy-done.2
  92.9 1.6 gather_fusion
  94.5 0.7 dynamic-slice_bitcast_fusion
  95.2 0.1 add_bitcast_fusion
  95.3 2.1 compare_and_fusion
  97.4 204.4 %all-to-all-done = bf16[64,128,576]{1,2,0:T(8,128)(2,1)} async-done(((bf16[64,128,576]{1,2,0:T(8,128)(2,1)}), bf16[64,128,576]{1,2,0:T(8,128)(2,1)}, u32[]{:S(2)}, u32[]{:S(2)}) %all-to-all-start) | async-done | bytes 9437216 | tf_op jit(solution)/shard_map/all_to_all | solution.py:30
  301.8 9.0 %fusion.11 = bf16[16,128,576]{1,0,2:T(8,128)(2,1)S(1)} fusion(bf16[64,128,576]{1,2,0:T(8,128)(2,1)} %all-to-all-done, s32[16]{0:T(128)S(1)} %get-tuple-element.8), kind=kOutput, calls=%fused_computation.18 | convolution fusion | flops 152175616 | bytes 11796544 | tf_op jit(solution)/shard_map/tn,nrd->trd/dot_general | solution.py:31
  310.8 2.4 reshape.152
  313.2 2.1 copy.22
  315.3 0.0 copy-done
  315.3 14.1 %fusion.37 = (f32[128,8]{0,1:T(8,128)S(1)}, f32[128,8,2048]{0,2,1:T(8,128)}) fusion(pred[128,2048]{0,1:T(8,128)(4,1)} %compare_and_fusion, bf16[2048,576,1]{0,1,2:T(8,128)(2,1)} %reshape.152, bf16[128,8,576]{0,2,1:T(8,128)(2,1)S(1)} %copy-done), kind=kOutput, calls=%fused_computation.57 | convolution fusion | flops 4844423168 | bytes 12193792 | tf_op jit(solution)/shard_map/sub | solution.py:48
  329.4 7.1 %fusion.16 = bf16[8,128,128]{1,2,0:T(8,128)(2,1)} fusion(bf16[8,512,128]{2,1,0:T(8,128)(2,1)} %param.9, bf16[2048,576]{0,1:T(8,128)(2,1)S(1)} %bitcast.61, f32[128,8,2048]{0,2,1:T(8,128)} %get-tuple-element.10, f32[128,8]{0,1:T(8,128)S(1)} %get-tuple-element.9), kind=kOutput, calls=%fused_computation.21 | convolution fusion | flops 2286551040 | bytes 11800576 | tf_op jit(solution)/shard_map/qhc,hcv->qhv/dot_general | solution.py:53
  336.5 1.8 copy.10
  (7 shorter events, 0.0 us)
Async XLA Ops:
  6.5 308.8 %copy-start = (bf16[128,8,576]{0,2,1:T(8,128)(2,1)S(1)}, bf16[128,8,576]{0,2,1:T(8,128)(2,1)}, u32[]{:S(2)}) copy-start(bf16[128,8,576]{0,2,1:T(8,128)(2,1)} %param.5) | copy-start | bytes 3538948
  6.5 52.4 %all-gather.3.cloned.1.call-start = ((), (), s32[]{:S(2)}) async-start(), calls=%async_computation.1 | async-start | bytes 2949120 | tf_op jit(solution)/shard_map/all_gather | solution.py:26
  81.4 11.4 %copy-start.2 = (s32[1,16]{1,0:T(1,128)S(1)}, s32[1,16]{1,0:T(1,128)}, u32[]{:S(2)}) copy-start(s32[1,16]{1,0:T(1,128)} %param.8) | copy-start | bytes 196
  81.4 220.3 %all-to-all-start = ((bf16[64,128,576]{1,2,0:T(8,128)(2,1)}), bf16[64,128,576]{1,2,0:T(8,128)(2,1)}, u32[]{:S(2)}, u32[]{:S(2)}) async-start(bf16[64,128,576]{1,2,0:T(8,128)(2,1)} %copy.21), calls=%async_computation | async-start | bytes 18874368 | tf_op jit(solution)/shard_map/all_to_all | solution.py:30
  315.3 14.1 %copy-start.1 = (bf16[72,8,16,128]{3,1,2,0:T(8,128)(2,1)S(1)}, bf16[72,8,16,128]{3,1,2,0:T(8,128)(2,1)}, u32[]{:S(2)}) copy-start(bf16[72,8,16,128]{3,1,2,0:T(8,128)(2,1)} %copy.22) | copy-start | bytes 7077892
Sparse Core Ops, SparseCore 0:
  9.4 49.4 all-gather.2
where the time goes:
time: 346 us; the launch traced here: 345 us
  waiting for transfers between devices  212 us (61%)
  blocking collectives  44.7 us (13%)
  matrix products  35.3 us (10%)
  local copies, waits for them, and re-layouts  26 us (8%)
  between operations  13.5 us (4%)
  starting transfers between devices  11.4 us (3%)
    all_to_all x1, waiting for transfers between devices, shards(): lax.all_to_all(outgoing, 'ctx', split_axis=0, concat_axis=0, tiled=True)  204 us
    all_gather x1, blocking collectives, shards(): requests = lax.all_gather(block_lists, 'ctx', axis=0, tiled=True)  44.7 us
    sub x1, matrix products, shards(): weights = jnp.where(allowed[:, None, :], jnp.exp(scores - row_max), 0.0)  14.1 us
    dot_general x1, local copies, waits for them, and re-layouts, shards(): jnp.einsum('nk,krd->nrd', chooser, whole, preferred_element_type=jnp.floa...  13.4 us
    all_to_all x1, starting transfers between devices, shards(): lax.all_to_all(outgoing, 'ctx', split_axis=0, concat_axis=0, tiled=True)  11.4 us
    dot_general x1, matrix products, shards(): jnp.einsum('tn,nrd->trd', picker, incoming, preferred_element_type=jnp.fl...  9.04 us
    dot_general x1, matrix products, shards(): jnp.einsum('qhc,hcv->qhv', latent_out, value_up, preferred_element_type=j...  7.09 us
  transfers between devices with their start and end apart: 2, of which 2 were waited for; matrix products, arithmetic and copies ran while one was open for 1% of the time, Pallas kernels for 0%

commit v1 on v0

v1 whole, which is shorter than its diff:
```python
import functools

import jax
import jax.numpy as jnp
from jax import lax
from jax.experimental import pallas as pl
from jax.experimental.pallas import tpu as pltpu
from jax.sharding import PartitionSpec as P

DC = 512
DR = 64
DN = 128
NEG = -1e30
EXP2_SCALE = (DN + DR) ** (-0.5) * 1.4426950408889634


def attention_kernel(q_ref, k_ref, vup_ref, bias_ref, o_ref, q32, qh, m_ref, l_ref, acc):
    heads = vup_ref.shape[0]
    tokens = q_ref.shape[0]
    chunks = k_ref.shape[0]
    rows = heads * tokens
    depth = q_ref.shape[2]
    for start in range(0, depth, 128):
        cols = min(128, depth - start)
        part = q_ref[:, :, start:start + cols].astype(jnp.float32).reshape(rows, cols)
        if cols < 128:
            part = jnp.concatenate([part, part], axis=1)
        q32[...] = part
        for h in range(heads):
            column = q32[pl.ds(h, tokens, stride=heads), :].astype(jnp.bfloat16)
            qh[h, :, start:start + cols] = column[:, :cols]
    m_ref[...] = jnp.full_like(m_ref, NEG)
    l_ref[...] = jnp.zeros_like(l_ref)
    acc[...] = jnp.zeros_like(acc)

    def one_chunk(c, carry):
        keys = k_ref[c]
        bias = bias_ref[c]
        for h in range(heads):
            s = lax.dot_general(
                qh[h], keys, (((1,), (1,)), ((), ())), preferred_element_type=jnp.float32
            )
            s = s + bias
            m_old = m_ref[h]
            m_new = jnp.maximum(m_old, jnp.max(s, axis=1, keepdims=True))
            alpha = jnp.exp2((m_old - m_new) * EXP2_SCALE)
            p = jnp.exp2((s - m_new[:, :1]) * EXP2_SCALE)
            half = p.shape[1] // 2
            l_ref[h] = l_ref[h] * alpha + (p[:, :half] + p[:, half:])
            m_ref[h] = m_new
            pv = jnp.dot(p.astype(jnp.bfloat16), keys[:, :DC], preferred_element_type=jnp.float32)
            acc[h] = acc[h] * alpha[:, :1] + pv
        return carry

    lax.fori_loop(0, chunks, one_chunk, 0)
    width = vup_ref.shape[2]
    for h in range(heads):
        total = jnp.sum(l_ref[h], axis=1, keepdims=True)
        latent = (acc[h] / total).astype(jnp.bfloat16)
        o_ref[:, h * width:(h + 1) * width] = jnp.dot(
            latent, vup_ref[h], preferred_element_type=jnp.float32
        ).astype(o_ref.dtype)


def attention(queries, keys, value_up, bias):
    tokens, heads, depth = queries.shape
    rows = tokens * heads
    vmem = pl.BlockSpec(memory_space=pltpu.VMEM)
    return pl.pallas_call(
        attention_kernel,
        out_shape=jax.ShapeDtypeStruct((tokens, heads * value_up.shape[2]), jnp.bfloat16),
        in_specs=[vmem] * 4,
        out_specs=vmem,
        scratch_shapes=[
            pltpu.VMEM((rows, 128), jnp.float32),
            pltpu.VMEM((heads, tokens, depth), jnp.bfloat16),
            pltpu.VMEM((heads, tokens, 128), jnp.float32),
            pltpu.VMEM((heads, tokens, 128), jnp.float32),
            pltpu.VMEM((heads, tokens, DC), jnp.float32),
        ],
        compiler_params=pltpu.CompilerParams(vmem_limit_bytes=40 * 1024 * 1024),
    )(queries, keys, value_up, bias)


def shards(queries, latent_cache, key_segments, block_lists, value_up):
    owners = lax.axis_size("ctx")
    own_index = lax.axis_index("ctx")
    depth, piece, width = latent_cache.shape
    pieces = lax.axis_size("tp")
    requests = lax.all_gather(block_lists, "ctx", axis=0, tiled=True)
    matched = requests % owners == own_index
    level = jnp.sum(jnp.where(matched, requests // owners, 0), axis=1)
    outgoing = latent_cache[level]
    incoming = lax.all_to_all(outgoing, "ctx", split_axis=0, concat_axis=0, tiled=True)
    wanted = block_lists[0]
    picked = incoming[wanted % owners]
    gathered = lax.all_gather(picked, "tp", axis=0)
    keys = gathered.reshape(pieces, -1, width)
    own_block = (depth - 1) * owners + own_index
    block_len = key_segments.shape[1]
    token = jnp.arange(block_len, dtype=jnp.int32)
    pos = wanted[:, None] * block_len + token[None, :]
    query_seg = key_segments[own_block, block_len - 1]
    in_rollout = key_segments[wanted] == query_seg
    allowed = in_rollout[None] & (pos[None] <= (own_block * block_len + token)[:, None, None])
    bias = jnp.where(allowed, 0.0, NEG).astype(jnp.float32)
    bias = bias.reshape(block_len, -1, pieces, piece).transpose(2, 0, 1, 3)
    bias = bias.reshape(pieces, block_len, -1)
    return attention(queries, keys, value_up, bias)


def solution(mesh):
    return jax.shard_map(
        shards,
        mesh=mesh,
        in_specs=(
            P("ctx", "tp", None),
            P(None, ("ctx", "tp"), None),
            P(),
            P("ctx", None),
            P("tp", None, None),
        ),
        out_specs=P("ctx", "tp"),
        check_vma=False,
    )
```

time: 346 us -> 184 us (0.53)
  the two profiles are of different devices: /device:TPU:2 before, /device:TPU:4 now
where the time goes in v1:
time: 184 us; the launch traced here: 183 us
  waiting for transfers between devices  71.6 us (39%)
  blocking collectives  44.1 us (24%)
  Pallas kernels  34.6 us (19%)
  between operations  13.5 us (7%)
  local copies, waits for them, and re-layouts  10 us (5%)
  starting transfers between devices  8.29 us (5%)
    all_gather x1, blocking collectives, shards(): requests = lax.all_gather(block_lists, 'ctx', axis=0, tiled=True)  44.1 us
    all_gather x1, waiting for transfers between devices, shards(): gathered = lax.all_gather(picked, 'tp', axis=0)  37.3 us
    pallas_call x1, Pallas kernels, attention(): pl.pallas_call(attention_kernel, out_shape=jax.ShapeDtypeStruct((tokens,...  34.6 us
    all_to_all x1, waiting for transfers between devices, shards(): lax.all_to_all(outgoing, 'ctx', split_axis=0, concat_axis=0, tiled=True)  34.3 us
    all_to_all x1, starting transfers between devices, shards(): lax.all_to_all(outgoing, 'ctx', split_axis=0, concat_axis=0, tiled=True)  8.24 us
    unnamed x11, local copies, waits for them, and re-layouts  4.34 us
  transfers between devices with their start and end apart: 2, of which 2 were waited for; matrix products, arithmetic and copies ran while one was open for 2% of the time, Pallas kernels for 0%

profile of v1, /device:TPU:4, one launch (start us, length us, event | category | flops | bytes accessed | tf_op | source)
XLA Modules:
  0.0 183.3 jit_solution(6336926378939601006)
XLA Ops:
  6.5 0.0 copy-start
  6.5 44.1 %all-gather.1 = s32[64,1,16]{2,1,0:T(1,128)S(1)} all-gather(s32[1,1,16]{2,1,0:T(1,128)} %bitcast.21), channel_id=1, replica_groups=mesh['ctx'=64,'tp'=8] {'ctx'}, dimensions={0}, use_global_device_ids=true | all-gather | bytes 4160 | tf_op jit(solution)/shard_map/all_gather | solution.py:90
  50.7 0.1 fusion.2
  50.8 2.7 %gather_fusion = bf16[64,16,576]{2,1,0:T(8,128)(2,1)} fusion(bf16[16,16,576]{2,1,0:T(8,128)(2,1)} %param.6, s32[1024]{0:T(1024)S(1)} %pad_clamp_fusion.2), kind=kCustom, calls=%fused_computation | custom fusion | bytes 2359552 | tf_op jit(solution)/shard_map/gather | solution.py:93
  53.6 8.2 %all-to-all-start = ((bf16[64,16,576]{2,1,0:T(8,128)(2,1)}), bf16[64,16,576]{2,1,0:T(8,128)(2,1)S(1)}, u32[]{:S(2)}, u32[]{:S(2)}) async-start(bf16[64,16,576]{2,1,0:T(8,128)(2,1)} %gather_fusion), calls=%async_computation | async-start | bytes 2621440 | tf_op jit(solution)/shard_map/all_to_all | solution.py:94
  61.8 0.0 copy-start.3
  61.9 0.0 all-gather.4.cloned.1.call-start
  61.9 34.3 %all-to-all-done = bf16[64,16,576]{2,1,0:T(8,128)(2,1)S(1)} async-done(((bf16[64,16,576]{2,1,0:T(8,128)(2,1)}), bf16[64,16,576]{2,1,0:T(8,128)(2,1)S(1)}, u32[]{:S(2)}, u32[]{:S(2)}) %all-to-all-start) | async-done | bytes 1179680 | tf_op jit(solution)/shard_map/all_to_all | solution.py:94
  96.3 1.3 gather_fusion.1
  97.6 0.0 all-gather.4.cloned.1.call-update
  97.6 0.6 constant_dynamic-slice_fusion
  98.2 0.6 gather_fusion.2
  98.8 0.1 add.111
  98.9 0.1 add.112
  98.9 0.7 broadcast_compare_fusion
  99.6 0.1 eq.27
  99.7 0.1 and.48
  99.8 0.1 add.120
  99.9 1.4 copy.9.q_ref
  101.3 0.2 and_select_fusion.bias_ref
  101.6 37.3 %all-gather.4.cloned.1.call-done = bf16[128,16,576]{2,1,0:T(8,128)(2,1)} async-done(((bf16[16,16,576]{2,1,0:T(8,128)(2,1)}), bf16[128,16,576]{2,1,0:T(8,128)(2,1)}) %all-gather.4.cloned.1.call-update) | async-done | bytes 2359312 | tf_op jit(solution)/shard_map/all_gather | solution.py:97
  138.8 1.7 copy-done.1
  140.6 1.2 copy-done.2
  141.8 34.6 %shard_map.55 = bf16[128,1024]{1,0:T(8,128)(2,1)} custom-call(bf16[128,8,576]{2,1,0:T(8,128)(2,1)S(1)} %copy.9.q_ref, bf16[8,256,576]{2,1,0:T(8,128)(2,1)S(1)} %bitcast.18, bf16[8,512,128]{2,1,0:T(8,128)(2,1)S(1)} %copy-done.2, f32[8,128,256]{2,1,0:T(8,128)S(1)} %and_select_fusion.bias_ref), custom_call_target="tpu_custom_call" | custom-call | tf_op jit(solution)/shard_map/pallas_call | solution.py:69
  (17 shorter events, 0.1 us)
Async XLA Ops:
  6.5 91.1 %copy-start = (s32[1024,128]{1,0:T(8,128)S(1)}, s32[1024,128]{1,0:T(8,128)}, u32[]{:S(2)}) copy-start(s32[1024,128]{1,0:T(8,128)} %param.7) | copy-start | bytes 1572868
  53.6 8.3 %copy-start.4 = (s32[1,16]{1,0:T(1,128)S(1)}, s32[1,16]{1,0:T(1,128)}, u32[]{:S(2)}) copy-start(s32[1,16]{1,0:T(1,128)} %param.8) | copy-start | bytes 196
  53.6 42.7 %all-to-all-start = ((bf16[64,16,576]{2,1,0:T(8,128)(2,1)}), bf16[64,16,576]{2,1,0:T(8,128)(2,1)S(1)}, u32[]{:S(2)}, u32[]{:S(2)}) async-start(bf16[64,16,576]{2,1,0:T(8,128)(2,1)} %gather_fusion), calls=%async_computation | async-start | bytes 2621440 | tf_op jit(solution)/shard_map/all_to_all | solution.py:94
  61.8 38.1 %copy-start.3 = (bf16[128,8,576]{0,2,1:T(8,128)(2,1)S(1)}, bf16[128,8,576]{0,2,1:T(8,128)(2,1)}, u32[]{:S(2)}) copy-start(bf16[128,8,576]{0,2,1:T(8,128)(2,1)} %param.5) | copy-start | bytes 3538948
  61.9 77.0 %all-gather.4.cloned.1.call-start = ((), (), s32[]{:S(2)}) async-start(), calls=%async_computation.1 | async-start | bytes 2949120 | tf_op jit(solution)/shard_map/all_gather | solution.py:97
  138.8 1.7 copy-start.1
  140.6 1.2 copy-start.2
Sparse Core Ops, SparseCore 0:
  97.7 41.0 all-gather.3

commit v2 on v0

v2 whole, which is shorter than its diff:
```python
import jax
import jax.numpy as jnp
from jax import lax
from jax.experimental import pallas as pl
from jax.experimental.pallas import tpu as pltpu
from jax.sharding import PartitionSpec as P

MESH = pl.DeviceIdType.MESH
DC = 512
DR = 64
DN = 128
BIG = 1e30
EXP2_SCALE = (DN + DR) ** (-0.5) * 1.4426950408889634
NZ, NX = 4, 8
CHIPS = NZ * NX
RING = 8
HEADS = 8
TOKENS = 128
PIECE = 16
LISTED = 16
LEVELS = 16
ROWS = HEADS * TOKENS
KEYS = LISTED * PIECE
LANES = 128
PARTS = 2
MESSAGE = (4, 5)
CHUNK = (32, 40)


def body(
    lists, cache, q_hbm, vup_hbm, seg_hbm, out,
    q_in, vup, seg, both, want_in, comb, levels,
    send_a, send_b, recv_a, recv_b, gat_a, gat_b,
    qa, kcat, valid, m_ref, l_ref, acc,
    local_sem, level_sem, sib_send, sib_recv, want_send, want_recv,
    mess_send, mess_recv, ring_send, ring_recv,
):
    me = lax.axis_index("ctx")
    t = lax.axis_index("tp")
    chip = me // 2
    core = me % 2
    z = chip // NX
    x = chip % NX
    right = (t + 1) % RING
    left = (t + RING - 1) % RING
    sends, recvs, gats = (send_a, send_b), (recv_a, recv_b), (gat_a, gat_b)

    def other(o):
        return ((z + o // NX) % NZ) * NX + (x + o % NX) % NX

    barrier = pltpu.get_barrier_semaphore()

    def greet(o, carry):
        pl.semaphore_signal(
            barrier, inc=1, device_id=(other(o) * 2 + core, t), device_id_type=MESH
        )
        return carry

    lax.fori_loop(1, CHIPS, greet, 0)
    for peer in ((chip * 2 + 1 - core, t), (me, right), (me, left)):
        pl.semaphore_signal(barrier, inc=1, device_id=peer, device_id_type=MESH)

    locals_ = [
        pltpu.make_async_copy(q_hbm, q_in, local_sem.at[0]),
        pltpu.make_async_copy(vup_hbm, vup, local_sem.at[1]),
        pltpu.make_async_copy(seg_hbm, seg, local_sem.at[2]),
    ]
    for copy in locals_:
        copy.start()

    lane8 = lax.broadcasted_iota(jnp.int32, (8, LANES), 1)
    row = jnp.zeros((8, LANES), jnp.int32)
    for j in range(LISTED):
        entry = lists[0, j]
        row = jnp.where(lane8 == (entry & 63), entry >> 6, row)
    want_in[chip] = row

    for level in range(LEVELS):
        for i in range(4):
            both[core, level, i] = cache[level, :, i * LANES:(i + 1) * LANES]
        rope = cache[level, :, DC:DC + DR]
        both[core, level, 4] = jnp.concatenate([rope, rope], axis=1)

    pl.semaphore_wait(barrier, CHIPS - 1 + 3)

    def want_copy(o):
        return pltpu.make_async_remote_copy(
            src_ref=want_in.at[chip], dst_ref=want_in.at[chip],
            send_sem=want_send.at[o], recv_sem=want_recv.at[chip],
            device_id=(other(o) * 2 + core, t), device_id_type=MESH,
        )

    def want_start(o, carry):
        want_copy(o).start()
        return carry

    lax.fori_loop(1, CHIPS, want_start, 0)
    sibling = pltpu.make_async_remote_copy(
        src_ref=both.at[core], dst_ref=both.at[core],
        send_sem=sib_send, recv_sem=sib_recv,
        device_id=(chip * 2 + 1 - core, t), device_id_type=MESH,
    )
    sibling.start()

    def want_wait(o, carry):
        source = other(o)
        pltpu.make_async_remote_copy(
            src_ref=want_in.at[source], dst_ref=want_in.at[source],
            send_sem=want_send.at[o], recv_sem=want_recv.at[source],
            device_id=(source * 2 + core, t), device_id_type=MESH,
        ).wait_recv()
        return carry

    lax.fori_loop(1, CHIPS, want_wait, 0)
    for s in range(CHIPS):
        comb[s:s + 1, :] = want_in[s, 0:1, :]
    to_scalar = pltpu.make_async_copy(comb, levels, level_sem)
    to_scalar.start()
    pltpu.make_async_remote_copy(
        src_ref=both.at[1 - core], dst_ref=both.at[1 - core],
        send_sem=sib_send, recv_sem=sib_recv,
        device_id=(chip * 2 + 1 - core, t), device_id_type=MESH,
    ).wait_recv()
    to_scalar.wait()

    lane16 = lax.broadcasted_iota(jnp.int32, (PIECE, LANES), 1)

    def fill(part, dest, ref, slot):
        at0 = levels[dest, 2 * chip]
        at1 = levels[dest, 2 * chip + 1]
        for i in range(2):
            ref[slot, i] = both[0, at0, 2 * part + i]
            ref[slot, 2 + i] = both[1, at1, 2 * part + i]
        if part == 1:
            ref[slot, 4] = jnp.where(lane16 < DR, both[0, at0, 4], both[1, at1, 4])

    def message(part, o):
        dest = other(o)
        return pltpu.make_async_remote_copy(
            src_ref=sends[part].at[o], dst_ref=recvs[part].at[chip],
            send_sem=mess_send.at[part, o], recv_sem=mess_recv.at[part, chip],
            device_id=(dest * 2 + core, t), device_id_type=MESH,
        )

    for part in range(PARTS):
        def send_one(o, carry, part=part):
            fill(part, other(o), sends[part], o)
            message(part, o).start()
            return carry

        lax.fori_loop(1, CHIPS, send_one, 0)
        fill(part, chip, recvs[part], chip)

    locals_[0].wait()
    for h in range(HEADS):
        rows = slice(h * TOKENS, (h + 1) * TOKENS)
        for i in range(4):
            qa[rows, i * LANES:(i + 1) * LANES] = q_in[h, i * LANES:(i + 1) * LANES, :].T
        rope = q_in[h, DC:DC + DR, :]
        qa[rows, DC:] = jnp.concatenate([rope, rope], axis=0).T

    locals_[2].wait()
    last = seg[pl.ds((LEVELS - 1) * CHIPS * 2 + me, 1), :]
    query_seg = last[:, LANES - 1:LANES]
    for j in range(LISTED):
        place = (j % 2) * (LISTED // 2) + j // 2
        rollout = seg[pl.ds(lists[0, j], 1), :]
        valid[place:place + 1, :] = jnp.where(rollout == query_seg, 1.0, 0.0)

    m_ref[...] = jnp.full_like(m_ref, -BIG)
    l_ref[...] = jnp.zeros_like(l_ref)
    acc[...] = jnp.zeros_like(acc)

    def wait_messages(part):
        def one(o, carry):
            source = other(o)
            pltpu.make_async_remote_copy(
                src_ref=sends[part].at[o], dst_ref=recvs[part].at[source],
                send_sem=mess_send.at[part, o], recv_sem=mess_recv.at[part, source],
                device_id=(source * 2 + core, t), device_id_type=MESH,
            ).wait_recv()
            return carry

        lax.fori_loop(1, CHIPS, one, 0)

    def pick(part):
        halves = []
        for j in range(LISTED):
            place = (j % 2) * (LISTED // 2) + j // 2
            residue = lists[0, j] & 63
            source = residue >> 1
            parity = residue & 1
            for i in range(2):
                gats[part][t, i * LISTED + place] = recvs[part][source, parity * 2 + i]
            if part == 1:
                tile = recvs[part][source, 4]
                low, high = tile[:, :DR], tile[:, DR:]
                halves.append(jnp.where(parity == 0, low, high))
                if j % 2 == 1:
                    gats[part][t, 2 * LISTED + j // 2] = jnp.concatenate(halves, axis=1)
                    halves = []

    def ring(part, direction, step, half):
        whole = CHUNK[part]
        origin = (t - step + 1 + RING) % RING if direction == 0 else (t + step - 1) % RING
        start, count = (0, whole) if not half else (direction * (whole // 2), whole // 2)
        piece = gats[part].at[origin, pl.ds(start, count)]
        return pltpu.make_async_remote_copy(
            src_ref=piece, dst_ref=piece,
            send_sem=ring_send.at[part, direction, step],
            recv_sem=ring_recv.at[part, direction, step],
            device_id=(me, right if direction == 0 else left), device_id_type=MESH,
        )

    def ring_wait(part, direction, step, half):
        whole = CHUNK[part]
        origin = (t - step + RING) % RING if direction == 0 else (t + step) % RING
        start, count = (0, whole) if not half else (direction * (whole // 2), whole // 2)
        piece = gats[part].at[origin, pl.ds(start, count)]
        pltpu.make_async_remote_copy(
            src_ref=piece, dst_ref=piece,
            send_sem=ring_send.at[part, direction, step],
            recv_sem=ring_recv.at[part, direction, step],
            device_id=(me, right if direction == 0 else left), device_id_type=MESH,
        ).wait_recv()

    def ring_advance(part, step):
        for direction in range(2):
            ring_wait(part, direction, step, False)

            @pl.when(step < 3)
            def _(direction=direction):
                ring(part, direction, step + 1, False).start()

            @pl.when(step == 3)
            def _(direction=direction):
                ring(part, direction, 4, True).start()

    wait_messages(0)
    pick(0)
    for direction in range(2):
        ring(0, direction, 1, False).start()

    def first_part(step, carry):
        ring_advance(0, step)
        return carry

    lax.fori_loop(1, 4, first_part, 0)
    wait_messages(1)
    pick(1)
    for direction in range(2):
        ring(1, direction, 1, False).start()
    for direction in range(2):
        ring_wait(0, direction, 4, True)

    lane_r = lax.broadcasted_iota(jnp.int32, (LISTED // 2 * PIECE, LANES), 1)

    def attend(origin):
        for i in range(2):
            for part in range(2):
                at = (2 * part + i) * LANES
                kcat[:, at:at + LANES] = gats[part][
                    origin, i * LISTED:(i + 1) * LISTED
                ].reshape(KEYS, LANES)
        rope = gat_b[origin, 2 * LISTED:].reshape(KEYS // 2, LANES)
        kcat[:KEYS // 2, DC:] = jnp.where(lane_r < DR, rope, jnp.zeros_like(rope))
        kcat[KEYS // 2:, DC:] = jnp.where(lane_r < DR, jnp.zeros_like(rope), rope)
        token = lax.broadcasted_iota(jnp.int32, (LANES, KEYS), 0)
        key = lax.broadcasted_iota(jnp.int32, (LANES, KEYS), 1)
        spread = jnp.where(token == origin * PIECE + key % PIECE, 1.0, 0.0).astype(jnp.bfloat16)
        seen = jnp.dot(valid[...].astype(jnp.bfloat16), spread, preferred_element_type=jnp.float32)
        place = lax.broadcasted_iota(jnp.int32, (LISTED, KEYS), 0)
        lane = lax.broadcasted_iota(jnp.int32, (LISTED, KEYS), 1)
        seen = jnp.sum(jnp.where(lane // PIECE == place, seen, 0.0), axis=0, keepdims=True)
        bias = jnp.broadcast_to((seen - 1.0) * BIG, (TOKENS, KEYS))
        query = lax.broadcasted_iota(jnp.int32, (TOKENS, KEYS), 0)
        column = lax.broadcasted_iota(jnp.int32, (TOKENS, KEYS), 1)
        later = (column < PIECE) & (origin * PIECE + column > query)
        bias = jnp.where(later, -BIG, bias)
        group = 4
        for g in range(HEADS // group):
            rows = pl.ds(g * group * TOKENS, group * TOKENS)
            s = lax.dot_general(
                qa[rows, :], kcat[...], (((1,), (1,)), ((), ())),
                preferred_element_type=jnp.float32,
            )
            s = (s.reshape(group, TOKENS, KEYS) + bias[None]).reshape(group * TOKENS, KEYS)
            m_old = m_ref[rows, :]
            m_new = jnp.maximum(m_old, jnp.max(s, axis=1, keepdims=True))
            alpha = jnp.exp2((m_old - m_new) * EXP2_SCALE)
            p = jnp.exp2((s - m_new[:, :1]) * EXP2_SCALE)
            l_ref[rows, :] = l_ref[rows, :] * alpha + (p[:, :LANES] + p[:, LANES:])
            m_ref[rows, :] = m_new
            pv = jnp.dot(
                p.astype(jnp.bfloat16), kcat[:, :DC], preferred_element_type=jnp.float32
            )
            acc[rows, :] = acc[rows, :] * alpha[:, :1] + pv

    def visit(n, carry):
        step = (n + 1) // 2

        @pl.when((n % 2 == 1) & (n < 7))
        def _():
            ring_advance(1, step)

        @pl.when(n == 7)
        def _():
            for direction in range(2):
                ring_wait(1, direction, 4, True)

        attend((t + RING + (1 - 2 * (n % 2)) * step) % RING)
        return carry

    lax.fori_loop(0, RING, visit, 0)

    locals_[1].wait()
    width = vup.shape[2]
    for h in range(HEADS):
        rows = pl.ds(h * TOKENS, TOKENS)
        total = jnp.sum(l_ref[rows, :], axis=1, keepdims=True)
        latent = (acc[rows, :] / total).astype(jnp.bfloat16)
        out[:, h * width:(h + 1) * width] = jnp.dot(
            latent, vup[h], preferred_element_type=jnp.float32
        ).astype(out.dtype)

    sibling.wait_send()

    def sent(o, carry):
        want_copy(o).wait_send()
        for part in range(PARTS):
            message(part, o).wait_send()
        return carry

    lax.fori_loop(1, CHIPS, sent, 0)
    for part in range(PARTS):
        for direction in range(2):
            for step in range(1, 5):
                ring(part, direction, step, step == 4).wait_send()


def shards(queries, latent_cache, key_segments, block_lists, value_up):
    tokens, heads, width = queries.shape
    bf16, f32 = jnp.bfloat16, jnp.float32
    tile = (PIECE, LANES)
    vmem = pl.BlockSpec(memory_space=pltpu.VMEM)
    anywhere = pl.BlockSpec(memory_space=pl.ANY)
    return pl.pallas_call(
        body,
        out_shape=jax.ShapeDtypeStruct((tokens, heads * value_up.shape[2]), bf16),
        in_specs=[pl.BlockSpec(memory_space=pltpu.SMEM), vmem, anywhere, anywhere, anywhere],
        out_specs=vmem,
        scratch_shapes=[
            pltpu.VMEM((heads, width, tokens), bf16),
            pltpu.VMEM(value_up.shape, bf16),
            pltpu.VMEM(key_segments.shape, jnp.int32),
            pltpu.VMEM((2, LEVELS, 5) + tile, bf16),
            pltpu.VMEM((CHIPS, 8, LANES), jnp.int32),
            pltpu.VMEM((CHIPS, LANES), jnp.int32),
            pltpu.SMEM((CHIPS, LANES), jnp.int32),
            pltpu.VMEM((CHIPS, MESSAGE[0]) + tile, bf16),
            pltpu.VMEM((CHIPS, MESSAGE[1]) + tile, bf16),
            pltpu.VMEM((CHIPS, MESSAGE[0]) + tile, bf16),
            pltpu.VMEM((CHIPS, MESSAGE[1]) + tile, bf16),
            pltpu.VMEM((RING, CHUNK[0]) + tile, bf16),
            pltpu.VMEM((RING, CHUNK[1]) + tile, bf16),
            pltpu.VMEM((ROWS, DC + LANES), bf16),
            pltpu.VMEM((KEYS, DC + LANES), bf16),
            pltpu.VMEM((LISTED, LANES), f32),
            pltpu.VMEM((ROWS, LANES), f32),
            pltpu.VMEM((ROWS, LANES), f32),
            pltpu.VMEM((ROWS, DC), f32),
            pltpu.SemaphoreType.DMA((3,)),
            pltpu.SemaphoreType.DMA,
            pltpu.SemaphoreType.DMA,
            pltpu.SemaphoreType.DMA,
            pltpu.SemaphoreType.DMA((CHIPS,)),
            pltpu.SemaphoreType.DMA((CHIPS,)),
            pltpu.SemaphoreType.DMA((PARTS, CHIPS)),
            pltpu.SemaphoreType.DMA((PARTS, CHIPS)),
            pltpu.SemaphoreType.DMA((PARTS, 2, 5)),
            pltpu.SemaphoreType.DMA((PARTS, 2, 5)),
        ],
        compiler_params=pltpu.CompilerParams(
            collective_id=0, has_side_effects=True, vmem_limit_bytes=60 * 1024 * 1024
        ),
    )(block_lists, latent_cache, queries.transpose(1, 2, 0), value_up, key_segments)


def solution(mesh):
    return jax.shard_map(
        shards,
        mesh=mesh,
        in_specs=(
            P("ctx", "tp", None),
            P(None, ("ctx", "tp"), None),
            P(),
            P("ctx", None),
            P("tp", None, None),
        ),
        out_specs=P("ctx", "tp"),
        check_vma=False,
    )
```

time: 346 us -> 87.4 us (0.25)
  waiting for transfers between devices: 212 us -> 0 us
  Pallas kernels: 0 us -> 85.5 us
  blocking collectives: 44.7 us -> 0 us
  matrix products: 35.3 us -> 0 us
  local copies, waits for them, and re-layouts: 26 us -> 1.67 us
  between operations: 13.5 us -> 0.01 us
  starting transfers between devices: 11.4 us -> 0 us
    all_to_all x1 -> x0, waiting for transfers between devices: 204 us -> none  [shards(): lax.all_to_all(outgoing, 'ctx', split_axis=0, concat_axis=0, tiled=True)]
    pallas_call x0 -> x1, Pallas kernels: none -> 85.5 us  [shards(): pl.pallas_call(body, out_shape=jax.ShapeDtypeStruct((tokens, heads * valu...]
    all_gather x1 -> x0, blocking collectives: 44.7 us -> none  [shards(): requests = lax.all_gather(block_lists, 'ctx', axis=0, tiled=True)]
    dot_general x3 -> x0, matrix products: 21.2 us -> none  [the longest x1 9.04 us: shards(): jnp.einsum('tn,nrd->trd', picker, incoming, preferred_element_type=jnp.fl...]
    sub x1 -> x0, matrix products: 14.1 us -> none  [shards(): weights = jnp.where(allowed[:, None, :], jnp.exp(scores - row_max), 0.0)]
    dot_general x1 -> x0, local copies, waits for them, and re-layouts: 13.4 us -> none  [shards(): jnp.einsum('nk,krd->nrd', chooser, whole, preferred_element_type=jnp.floa...]
    all_to_all x1 -> x0, starting transfers between devices: 11.4 us -> none  [shards(): lax.all_to_all(outgoing, 'ctx', split_axis=0, concat_axis=0, tiled=True)]
    all_gather x1 -> x0, waiting for transfers between devices: 6.72 us -> none  [shards(): whole = lax.all_gather(latent_cache, 'tp', axis=1, tiled=True)]
  transfers between devices with their start and end apart: 2 -> 0, of which waited for: 2 -> 0; matrix products, arithmetic and copies ran while one was open for 1% -> 0% of each run, Pallas kernels for 0% -> 0%
where the time goes in v2:
time: 87.4 us; the launch traced here: 87.2 us
  Pallas kernels  85.5 us (98%)
  local copies, waits for them, and re-layouts  1.67 us (2%)
    pallas_call x1, Pallas kernels, shards(): pl.pallas_call(body, out_shape=jax.ShapeDtypeStruct((tokens, heads * valu...  85.5 us

profile of v2, /device:TPU:2, one launch (start us, length us, event | category | flops | bytes accessed | tf_op | source)
XLA Modules:
  0.0 87.2 jit_solution(6033990054167659591)
XLA Ops:
  0.0 85.5 %shard_map.55 = bf16[128,1024]{1,0:T(8,128)(2,1)} custom-call(s32[1,16]{1,0:T(1,128)} %lists.1, bf16[16,16,576]{2,1,0:T(8,128)(2,1)} %cache.1, bf16[8,576,128]{2,1,0:T(8,128)(2,1)} %bitcast.1, bf16[8,512,128]{2,1,0:T(8,128)(2,1)} %vup_hbm.1, s32[1024,128]{1,0:T(8,128)} %seg_hbm.1), custom_call_target="tpu_custom_call" | custom-call | tf_op jit(solution)/shard_map/pallas_call | solution.py:347
  85.5 1.7 %copy.7 = bf16[128,1024]{1,0:T(8,128)(2,1)} copy(bf16[128,1024]{1,0:T(8,128)(2,1)} %shard_map.55) | data formatting | bytes 524288

commit v3 on v0

v3 whole, which is shorter than its diff:
```python
import jax
import jax.numpy as jnp
from jax import lax
from jax.experimental import pallas as pl
from jax.experimental.pallas import tpu as pltpu
from jax.sharding import PartitionSpec as P

MESH = pl.DeviceIdType.MESH
DC = 512
DR = 64
DN = 128
BIG = 1e30
EXP2_SCALE = (DN + DR) ** (-0.5) * 1.4426950408889634
NZ, NX = 4, 8
GROUP = 2 * NX
RING = 8
HEADS = 8
TOKENS = 128
PIECE = 16
LISTED = 16
LEVELS = 16
ROWS = HEADS * TOKENS
KEYS = LISTED * PIECE
LANES = 128
PARTS = 4
ROPE = 1
BATCH = 4
SHARD = tuple(24 if part == ROPE else 16 for part in range(PARTS))
MESSAGE = tuple(6 if part == ROPE else 4 for part in range(PARTS))
CHUNK = SHARD


def body(
    lists, cache, q_hbm, vup_hbm, seg_hbm, out, *scratch
):
    planes, sends, recvs, gats = (scratch[PARTS * i:PARTS * (i + 1)] for i in range(4))
    (
        q_in, vup, seg, want_in, comb, levels,
        qa, kcat, valid, m_ref, l_ref, acc,
        local_sem, level_sem, want_send, want_recv, plane_send, plane_recv,
        mess_send, mess_recv, ring_send, ring_recv,
    ) = scratch[4 * PARTS:]
    me = lax.axis_index("ctx")
    t = lax.axis_index("tp")
    z = me // GROUP
    spot = me % GROUP
    x = spot // 2
    core = spot % 2
    right = (t + 1) % RING
    left = (t + RING - 1) % RING
    above = ((z + 1) % NZ) * GROUP + spot
    below = ((z + NZ - 1) % NZ) * GROUP + spot

    def other(o):
        return ((x + o // 2) % NX) * 2 + (core + o % 2) % 2

    barrier = pltpu.get_barrier_semaphore()
    for peer in ((above, t), (below, t), (me, right), (me, left)):
        pl.semaphore_signal(barrier, inc=1, device_id=peer, device_id_type=MESH)

    def greet(o, carry):
        pl.semaphore_signal(
            barrier, inc=1, device_id=(z * GROUP + other(o), t), device_id_type=MESH
        )
        return carry

    lax.fori_loop(1, GROUP, greet, 0)

    locals_ = [
        pltpu.make_async_copy(q_hbm, q_in, local_sem.at[0]),
        pltpu.make_async_copy(vup_hbm, vup, local_sem.at[1]),
        pltpu.make_async_copy(seg_hbm, seg, local_sem.at[2]),
    ]
    for copy in locals_:
        copy.start()

    lane8 = lax.broadcasted_iota(jnp.int32, (8, LANES), 1)
    row = jnp.zeros((8, LANES), jnp.int32)
    for j in range(LISTED):
        entry = lists[0, j]
        row = jnp.where(lane8 == (entry & 63), entry >> 6, row)
    want_in[spot] = row

    for level in range(LEVELS):
        for part in range(PARTS):
            planes[part][z, level] = cache[level, :, part * LANES:(part + 1) * LANES]
        if level % 2 == 1:
            planes[ROPE][z, LEVELS + level // 2] = jnp.concatenate(
                [cache[level - 1, :, DC:], cache[level, :, DC:]], axis=1
            )

    def plane_copy(part, direction, step, arriving):
        whole = SHARD[part]
        hops = step if arriving else step - 1
        origin = (z + NZ - hops) % NZ if direction == 0 else (z + hops) % NZ
        start, count = (0, whole) if step == 1 else (direction * (whole // 2), whole // 2)
        piece = planes[part].at[origin, pl.ds(start, count)]
        return pltpu.make_async_remote_copy(
            src_ref=piece, dst_ref=piece,
            send_sem=plane_send.at[part, direction, step],
            recv_sem=plane_recv.at[part, direction, step],
            device_id=(above if direction == 0 else below, t), device_id_type=MESH,
        )

    pl.semaphore_wait(barrier, GROUP - 1 + 4)

    def want_copy(o):
        return pltpu.make_async_remote_copy(
            src_ref=want_in.at[spot], dst_ref=want_in.at[spot],
            send_sem=want_send.at[o], recv_sem=want_recv.at[spot],
            device_id=(z * GROUP + other(o), t), device_id_type=MESH,
        )

    def want_start(o, carry):
        want_copy(o).start()
        return carry

    def plane_open(part):
        for direction in range(2):
            plane_copy(part, direction, 1, False).start()

    plane_open(0)
    lax.fori_loop(1, GROUP, want_start, 0)
    plane_open(1)

    locals_[0].wait()
    for h in range(HEADS):
        rows = slice(h * TOKENS, (h + 1) * TOKENS)
        for i in range(4):
            qa[rows, i * LANES:(i + 1) * LANES] = q_in[h, i * LANES:(i + 1) * LANES, :].T
        rope = q_in[h, DC:DC + DR, :]
        qa[rows, DC:] = jnp.concatenate([rope, rope], axis=0).T

    def plane_pass(part):
        for direction in range(2):
            plane_copy(part, direction, 1, True).wait_recv()
            plane_copy(part, direction, 2, False).start()

    plane_pass(0)
    plane_open(2)

    def want_wait(o, carry):
        source = other(o)
        pltpu.make_async_remote_copy(
            src_ref=want_in.at[source], dst_ref=want_in.at[source],
            send_sem=want_send.at[o], recv_sem=want_recv.at[source],
            device_id=(z * GROUP + source, t), device_id_type=MESH,
        ).wait_recv()
        return carry

    lax.fori_loop(1, GROUP, want_wait, 0)
    for s in range(GROUP):
        comb[s:s + 1, :] = want_in[s, 0:1, :]
    to_scalar = pltpu.make_async_copy(comb, levels, level_sem)
    to_scalar.start()
    to_scalar.wait()

    def fill(part, dest, ref, slot):
        halves = []
        for plane in range(NZ):
            level = levels[dest, plane * GROUP + spot]
            ref[slot, plane] = planes[part][plane, level]
            if part == ROPE:
                tile = planes[part][plane, LEVELS + (level >> 1)]
                halves.append(jnp.where((level & 1) == 0, tile[:, :DR], tile[:, DR:]))
                if plane % 2 == 1:
                    ref[slot, NZ + plane // 2] = jnp.concatenate(halves, axis=1)
                    halves = []

    def message(part, o):
        return pltpu.make_async_remote_copy(
            src_ref=sends[part].at[o], dst_ref=recvs[part].at[spot],
            send_sem=mess_send.at[part, o], recv_sem=mess_recv.at[part, spot],
            device_id=(z * GROUP + other(o), t), device_id_type=MESH,
        )

    def plane_close(part):
        for direction in range(2):
            plane_copy(part, direction, 2, True).wait_recv()

        def send_one(o, carry):
            fill(part, other(o), sends[part], o)
            message(part, o).start()
            return carry

        lax.fori_loop(1, GROUP, send_one, 0)
        fill(part, spot, recvs[part], spot)

    locals_[2].wait()
    last = seg[pl.ds((LEVELS - 1) * NZ * GROUP + me, 1), :]
    query_seg = last[:, LANES - 1:LANES]
    for j in range(LISTED):
        place = (j % 2) * (LISTED // 2) + j // 2
        rollout = seg[pl.ds(lists[0, j], 1), :]
        valid[place:place + 1, :] = jnp.where(rollout == query_seg, 1.0, 0.0)

    m_ref[...] = jnp.full_like(m_ref, -BIG)
    l_ref[...] = jnp.zeros_like(l_ref)
    acc[...] = jnp.zeros_like(acc)

    def wait_messages(part):
        def one(o, carry):
            source = other(o)
            pltpu.make_async_remote_copy(
                src_ref=sends[part].at[o], dst_ref=recvs[part].at[source],
                send_sem=mess_send.at[part, o], recv_sem=mess_recv.at[part, source],
                device_id=(z * GROUP + source, t), device_id_type=MESH,
            ).wait_recv()
            return carry

        lax.fori_loop(1, GROUP, one, 0)

    def pick(part):
        halves = []
        for j in range(LISTED):
            place = (j % 2) * (LISTED // 2) + j // 2
            residue = lists[0, j] & 63
            plane = residue >> 4
            source = residue & 15
            gats[part][t, place] = recvs[part][source, plane]
            if part == ROPE:
                tile = recvs[part][source, NZ + (plane >> 1)]
                halves.append(jnp.where((plane & 1) == 0, tile[:, :DR], tile[:, DR:]))
                if j % 2 == 1:
                    gats[part][t, LISTED + j // 2] = jnp.concatenate(halves, axis=1)
                    halves = []

    def ring(part, direction, step, arriving):
        whole = CHUNK[part]
        hops = step if arriving else step - 1
        origin = (t + RING - hops) % RING if direction == 0 else (t + hops) % RING
        start, count = (0, whole) if step < 4 else (direction * (whole // 2), whole // 2)
        piece = gats[part].at[origin, pl.ds(start, count)]
        return pltpu.make_async_remote_copy(
            src_ref=piece, dst_ref=piece,
            send_sem=ring_send.at[part, direction, step],
            recv_sem=ring_recv.at[part, direction, step],
            device_id=(me, right if direction == 0 else left), device_id_type=MESH,
        )

    def ring_open(part):
        wait_messages(part)
        pick(part)
        for direction in range(2):
            ring(part, direction, 1, False).start()

    def ring_pass(part, step):
        for direction in range(2):
            ring(part, direction, step, True).wait_recv()
            if step < 4:
                ring(part, direction, step + 1, False).start()

    lane_r = lax.broadcasted_iota(jnp.int32, (KEYS // 2, LANES), 1)

    def attend(origins):
        count = len(origins) * KEYS
        biases = []
        for n, origin in enumerate(origins):
            first = slice(n * KEYS, n * KEYS + KEYS // 2)
            second = slice(n * KEYS + KEYS // 2, (n + 1) * KEYS)
            for part in range(PARTS):
                kcat[n * KEYS:(n + 1) * KEYS, part * LANES:(part + 1) * LANES] = gats[part][
                    origin, :LISTED
                ].reshape(KEYS, LANES)
            rope = gats[ROPE][origin, LISTED:].reshape(KEYS // 2, LANES)
            kcat[first, DC:] = jnp.where(lane_r < DR, rope, jnp.zeros_like(rope))
            kcat[second, DC:] = jnp.where(lane_r < DR, jnp.zeros_like(rope), rope)
            token = lax.broadcasted_iota(jnp.int32, (LANES, KEYS), 0)
            key = lax.broadcasted_iota(jnp.int32, (LANES, KEYS), 1)
            spread = jnp.where(token == origin * PIECE + key % PIECE, 1.0, 0.0).astype(jnp.bfloat16)
            seen = jnp.dot(
                valid[...].astype(jnp.bfloat16), spread, preferred_element_type=jnp.float32
            )
            place = lax.broadcasted_iota(jnp.int32, (LISTED, KEYS), 0)
            lane = lax.broadcasted_iota(jnp.int32, (LISTED, KEYS), 1)
            seen = jnp.sum(jnp.where(lane // PIECE == place, seen, 0.0), axis=0, keepdims=True)
            bias = jnp.broadcast_to((seen - 1.0) * BIG, (TOKENS, KEYS))
            query = lax.broadcasted_iota(jnp.int32, (TOKENS, KEYS), 0)
            column = lax.broadcasted_iota(jnp.int32, (TOKENS, KEYS), 1)
            later = (column < PIECE) & (origin * PIECE + column > query)
            biases.append(jnp.where(later, -BIG, bias))
        bias = jnp.concatenate(biases, axis=1) if len(origins) > 1 else biases[0]
        for g in range(HEADS // BATCH):
            rows = pl.ds(g * BATCH * TOKENS, BATCH * TOKENS)
            s = lax.dot_general(
                qa[rows, :], kcat[:count, :], (((1,), (1,)), ((), ())),
                preferred_element_type=jnp.float32,
            )
            s = (s.reshape(BATCH, TOKENS, count) + bias[None]).reshape(BATCH * TOKENS, count)
            m_old = m_ref[rows, :]
            m_new = jnp.maximum(m_old, jnp.max(s, axis=1, keepdims=True))
            alpha = jnp.exp2((m_old - m_new) * EXP2_SCALE)
            p = jnp.exp2((s - m_new[:, :1]) * EXP2_SCALE)
            l_new = l_ref[rows, :] * alpha
            for at in range(0, count, LANES):
                l_new = l_new + p[:, at:at + LANES]
            l_ref[rows, :] = l_new
            m_ref[rows, :] = m_new
            pv = jnp.dot(
                p.astype(jnp.bfloat16), kcat[:count, :DC], preferred_element_type=jnp.float32
            )
            acc[rows, :] = acc[rows, :] * alpha[:, :1] + pv

    for act, part, step in (
        (plane_close, 0, 0), (plane_pass, 1, 0), (plane_open, 3, 0), (plane_pass, 2, 0),
        (plane_close, 1, 0), (ring_open, 0, 0), (plane_pass, 3, 0), (plane_close, 2, 0),
        (ring_pass, 0, 1), (plane_close, 3, 0), (ring_open, 1, 0), (ring_pass, 0, 2),
        (ring_open, 2, 0), (ring_pass, 0, 3), (ring_pass, 1, 1), (ring_open, 3, 0),
        (ring_pass, 2, 1), (ring_pass, 1, 2), (ring_pass, 3, 1),
    ):
        act(part, step) if act is ring_pass else act(part)
    attend([t])
    for part, step in ((0, 4), (2, 2), (1, 3), (3, 2)):
        ring_pass(part, step)
    attend([left, right])
    for part, step in ((2, 3), (3, 3)):
        ring_pass(part, step)
    attend([(t + 6) % RING, (t + 2) % RING])
    for part, step in ((1, 4), (2, 4), (3, 4)):
        ring_pass(part, step)
    attend([(t + 5) % RING, (t + 3) % RING])
    attend([(t + 4) % RING])

    locals_[1].wait()
    width = vup.shape[2]
    for h in range(HEADS):
        rows = pl.ds(h * TOKENS, TOKENS)
        total = jnp.sum(l_ref[rows, :], axis=1, keepdims=True)
        latent = (acc[rows, :] / total).astype(jnp.bfloat16)
        out[:, h * width:(h + 1) * width] = jnp.dot(
            latent, vup[h], preferred_element_type=jnp.float32
        ).astype(out.dtype)

    def sent(o, carry):
        want_copy(o).wait_send()
        for part in range(PARTS):
            message(part, o).wait_send()
        return carry

    lax.fori_loop(1, GROUP, sent, 0)
    for part in range(PARTS):
        for direction in range(2):
            for step in range(1, 3):
                plane_copy(part, direction, step, False).wait_send()
            for step in range(1, 5):
                ring(part, direction, step, False).wait_send()


def shards(queries, latent_cache, key_segments, block_lists, value_up):
    tokens, heads, width = queries.shape
    bf16, f32 = jnp.bfloat16, jnp.float32
    vmem = pl.BlockSpec(memory_space=pltpu.VMEM)
    anywhere = pl.BlockSpec(memory_space=pl.ANY)

    def tiles(outer, counts):
        return [pltpu.VMEM((outer, count, PIECE, LANES), bf16) for count in counts]

    sem = pltpu.SemaphoreType.DMA
    return pl.pallas_call(
        body,
        out_shape=jax.ShapeDtypeStruct((tokens, heads * value_up.shape[2]), bf16),
        in_specs=[pl.BlockSpec(memory_space=pltpu.SMEM), vmem, anywhere, anywhere, anywhere],
        out_specs=vmem,
        scratch_shapes=[
            *tiles(NZ, SHARD),
            *tiles(GROUP, MESSAGE),
            *tiles(GROUP, MESSAGE),
            *tiles(RING, CHUNK),
            pltpu.VMEM((heads, width, tokens), bf16),
            pltpu.VMEM(value_up.shape, bf16),
            pltpu.VMEM(key_segments.shape, jnp.int32),
            pltpu.VMEM((GROUP, 8, LANES), jnp.int32),
            pltpu.VMEM((GROUP, LANES), jnp.int32),
            pltpu.SMEM((GROUP, LANES), jnp.int32),
            pltpu.VMEM((ROWS, DC + LANES), bf16),
            pltpu.VMEM((2 * KEYS, DC + LANES), bf16),
            pltpu.VMEM((LISTED, LANES), f32),
            pltpu.VMEM((ROWS, LANES), f32),
            pltpu.VMEM((ROWS, LANES), f32),
            pltpu.VMEM((ROWS, DC), f32),
            sem((3,)),
            sem,
            sem((GROUP,)),
            sem((GROUP,)),
            sem((PARTS, 2, 3)),
            sem((PARTS, 2, 3)),
            sem((PARTS, GROUP)),
            sem((PARTS, GROUP)),
            sem((PARTS, 2, 5)),
            sem((PARTS, 2, 5)),
        ],
        compiler_params=pltpu.CompilerParams(
            collective_id=0, has_side_effects=True, vmem_limit_bytes=60 * 1024 * 1024
        ),
    )(block_lists, latent_cache, queries.transpose(1, 2, 0), value_up, key_segments)


def solution(mesh):
    return jax.shard_map(
        shards,
        mesh=mesh,
        in_specs=(
            P("ctx", "tp", None),
            P(None, ("ctx", "tp"), None),
            P(),
            P("ctx", None),
            P("tp", None, None),
        ),
        out_specs=P("ctx", "tp"),
        check_vma=False,
    )
```

time: 346 us -> 81.1 us (0.23)
  waiting for transfers between devices: 212 us -> 0 us
  Pallas kernels: 0 us -> 79.2 us
  blocking collectives: 44.7 us -> 0 us
  matrix products: 35.3 us -> 0 us
  local copies, waits for them, and re-layouts: 26 us -> 1.67 us
  between operations: 13.5 us -> 0.01 us
  starting transfers between devices: 11.4 us -> 0 us
    all_to_all x1 -> x0, waiting for transfers between devices: 204 us -> none  [shards(): lax.all_to_all(outgoing, 'ctx', split_axis=0, concat_axis=0, tiled=True)]
    pallas_call x0 -> x1, Pallas kernels: none -> 79.2 us  [shards(): pl.pallas_call(body, out_shape=jax.ShapeDtypeStruct((tokens, heads * valu...]
    all_gather x1 -> x0, blocking collectives: 44.7 us -> none  [shards(): requests = lax.all_gather(block_lists, 'ctx', axis=0, tiled=True)]
    dot_general x3 -> x0, matrix products: 21.2 us -> none  [the longest x1 9.04 us: shards(): jnp.einsum('tn,nrd->trd', picker, incoming, preferred_element_type=jnp.fl...]
    sub x1 -> x0, matrix products: 14.1 us -> none  [shards(): weights = jnp.where(allowed[:, None, :], jnp.exp(scores - row_max), 0.0)]
    dot_general x1 -> x0, local copies, waits for them, and re-layouts: 13.4 us -> none  [shards(): jnp.einsum('nk,krd->nrd', chooser, whole, preferred_element_type=jnp.floa...]
    all_to_all x1 -> x0, starting transfers between devices: 11.4 us -> none  [shards(): lax.all_to_all(outgoing, 'ctx', split_axis=0, concat_axis=0, tiled=True)]
    all_gather x1 -> x0, waiting for transfers between devices: 6.72 us -> none  [shards(): whole = lax.all_gather(latent_cache, 'tp', axis=1, tiled=True)]
  transfers between devices with their start and end apart: 2 -> 0, of which waited for: 2 -> 0; matrix products, arithmetic and copies ran while one was open for 1% -> 0% of each run, Pallas kernels for 0% -> 0%
where the time goes in v3:
time: 81.1 us; the launch traced here: 80.9 us
  Pallas kernels  79.2 us (98%)
  local copies, waits for them, and re-layouts  1.67 us (2%)
    pallas_call x1, Pallas kernels, shards(): pl.pallas_call(body, out_shape=jax.ShapeDtypeStruct((tokens, heads * valu...  79.2 us
    unnamed x1, local copies, waits for them, and re-layouts  1.67 us

profile of v3, /device:TPU:2, one launch (start us, length us, event | category | flops | bytes accessed | tf_op | source)
XLA Modules:
  0.0 80.9 jit_solution(17258713259900883583)
XLA Ops:
  0.0 79.2 %shard_map.55 = bf16[128,1024]{1,0:T(8,128)(2,1)} custom-call(s32[1,16]{1,0:T(1,128)} %lists.1, bf16[16,16,576]{2,1,0:T(8,128)(2,1)} %cache.1, bf16[8,576,128]{2,1,0:T(8,128)(2,1)} %bitcast.1, bf16[8,512,128]{2,1,0:T(8,128)(2,1)} %vup_hbm.1, s32[1024,128]{1,0:T(8,128)} %seg_hbm.1), custom_call_target="tpu_custom_call" | custom-call | tf_op jit(solution)/shard_map/pallas_call | solution.py:359
  79.2 1.7 %copy.7 = bf16[128,1024]{1,0:T(8,128)(2,1)} copy(bf16[128,1024]{1,0:T(8,128)(2,1)} %shard_map.55) | data formatting | bytes 524288

commit v4 on v3

--- a/solution.py
+++ b/solution.py
@@ -24,7 +24,7 @@
 LANES = 128
 PARTS = 4
 ROPE = 1
-BATCH = 4
+BATCH = 2
 SHARD = tuple(24 if part == ROPE else 16 for part in range(PARTS))
 MESSAGE = tuple(6 if part == ROPE else 4 for part in range(PARTS))
 CHUNK = SHARD
@@ -301,24 +301,38 @@
             )
             acc[rows, :] = acc[rows, :] * alpha[:, :1] + pv
 
-    for act, part, step in (
-        (plane_close, 0, 0), (plane_pass, 1, 0), (plane_open, 3, 0), (plane_pass, 2, 0),
-        (plane_close, 1, 0), (ring_open, 0, 0), (plane_pass, 3, 0), (plane_close, 2, 0),
-        (ring_pass, 0, 1), (plane_close, 3, 0), (ring_open, 1, 0), (ring_pass, 0, 2),
-        (ring_open, 2, 0), (ring_pass, 0, 3), (ring_pass, 1, 1), (ring_open, 3, 0),
-        (ring_pass, 2, 1), (ring_pass, 1, 2), (ring_pass, 3, 1),
-    ):
-        act(part, step) if act is ring_pass else act(part)
+    plane_close(0)
+    plane_pass(1)
+    plane_open(3)
+    plane_pass(2)
+    plane_close(1)
+    ring_open(0)
+    plane_pass(3)
+    plane_close(2)
+    ring_pass(0, 1)
+    plane_close(3)
+    ring_open(1)
+    ring_pass(0, 2)
+    ring_open(2)
+    ring_pass(1, 1)
+    ring_open(3)
+    ring_pass(0, 3)
+    ring_pass(2, 1)
     attend([t])
-    for part, step in ((0, 4), (2, 2), (1, 3), (3, 2)):
-        ring_pass(part, step)
+    ring_pass(3, 1)
+    ring_pass(1, 2)
     attend([left, right])
-    for part, step in ((2, 3), (3, 3)):
-        ring_pass(part, step)
+    ring_pass(2, 2)
+    ring_pass(3, 2)
+    ring_pass(1, 3)
     attend([(t + 6) % RING, (t + 2) % RING])
-    for part, step in ((1, 4), (2, 4), (3, 4)):
-        ring_pass(part, step)
+    ring_pass(2, 3)
+    ring_pass(3, 3)
     attend([(t + 5) % RING, (t + 3) % RING])
+    ring_pass(0, 4)
+    ring_pass(1, 4)
+    ring_pass(2, 4)
+    ring_pass(3, 4)
     attend([(t + 4) % RING])
 
     locals_[1].wait()

time: 81.1 us -> 77.3 us (0.953)
  the two profiles are of different devices: /device:TPU:2 before, /device:TPU:66 now
where the time goes in v4:
time: 77.3 us; the launch traced here: 77.1 us
  Pallas kernels  75.4 us (98%)
  local copies, waits for them, and re-layouts  1.67 us (2%)
    pallas_call x1, Pallas kernels, shards(): pl.pallas_call(body, out_shape=jax.ShapeDtypeStruct((tokens, heads * valu...  75.4 us
    unnamed x1, local copies, waits for them, and re-layouts  1.67 us

profile of v4, /device:TPU:66, one launch (start us, length us, event | category | flops | bytes accessed | tf_op | source)
XLA Modules:
  0.0 77.1 jit_solution(14083097559997457772)
XLA Ops:
  0.0 75.4 %shard_map.55 = bf16[128,1024]{1,0:T(8,128)(2,1)} custom-call(s32[1,16]{1,0:T(1,128)} %lists.1, bf16[16,16,576]{2,1,0:T(8,128)(2,1)} %cache.1, bf16[8,576,128]{2,1,0:T(8,128)(2,1)} %bitcast.1, bf16[8,512,128]{2,1,0:T(8,128)(2,1)} %vup_hbm.1, s32[1024,128]{1,0:T(8,128)} %seg_hbm.1), custom_call_target="tpu_custom_call" | custom-call | tf_op jit(solution)/shard_map/pallas_call | solution.py:373
  75.5 1.7 %copy.7 = bf16[128,1024]{1,0:T(8,128)(2,1)} copy(bf16[128,1024]{1,0:T(8,128)(2,1)} %shard_map.55) | data formatting | bytes 524288

commit v5 on v4

--- a/solution.py
+++ b/solution.py
@@ -305,18 +305,18 @@
     plane_pass(1)
     plane_open(3)
     plane_pass(2)
+    ring_open(0)
     plane_close(1)
-    ring_open(0)
     plane_pass(3)
+    ring_pass(0, 1)
     plane_close(2)
-    ring_pass(0, 1)
+    ring_pass(0, 2)
     plane_close(3)
     ring_open(1)
-    ring_pass(0, 2)
+    ring_pass(0, 3)
     ring_open(2)
     ring_pass(1, 1)
     ring_open(3)
-    ring_pass(0, 3)
     ring_pass(2, 1)
     attend([t])
     ring_pass(3, 1)

time: 77.3 us -> 77.3 us (level)
  the two profiles are of different devices: /device:TPU:66 before, /device:TPU:8 now
where the time goes in v5:
time: 77.3 us; the launch traced here: 77.1 us
  Pallas kernels  75.5 us (98%)
  local copies, waits for them, and re-layouts  1.67 us (2%)
    pallas_call x1, Pallas kernels, shards(): pl.pallas_call(body, out_shape=jax.ShapeDtypeStruct((tokens, heads * valu...  75.5 us
    unnamed x1, local copies, waits for them, and re-layouts  1.67 us

profile of v5, /device:TPU:8, one launch (start us, length us, event | category | flops | bytes accessed | tf_op | source)
XLA Modules:
  0.0 77.1 jit_solution(10623015175884215618)
XLA Ops:
  0.0 75.5 %shard_map.55 = bf16[128,1024]{1,0:T(8,128)(2,1)} custom-call(s32[1,16]{1,0:T(1,128)} %lists.1, bf16[16,16,576]{2,1,0:T(8,128)(2,1)} %cache.1, bf16[8,576,128]{2,1,0:T(8,128)(2,1)} %bitcast.1, bf16[8,512,128]{2,1,0:T(8,128)(2,1)} %vup_hbm.1, s32[1024,128]{1,0:T(8,128)} %seg_hbm.1), custom_call_target="tpu_custom_call" | custom-call | tf_op jit(solution)/shard_map/pallas_call | solution.py:373
  75.5 1.7 %copy.7 = bf16[128,1024]{1,0:T(8,128)(2,1)} copy(bf16[128,1024]{1,0:T(8,128)(2,1)} %shard_map.55) | data formatting | bytes 524288

commit v6 on v4

--- a/solution.py
+++ b/solution.py
@@ -321,12 +321,12 @@
     attend([t])
     ring_pass(3, 1)
     ring_pass(1, 2)
+    ring_pass(2, 2)
     attend([left, right])
-    ring_pass(2, 2)
     ring_pass(3, 2)
     ring_pass(1, 3)
+    ring_pass(2, 3)
     attend([(t + 6) % RING, (t + 2) % RING])
-    ring_pass(2, 3)
     ring_pass(3, 3)
     attend([(t + 5) % RING, (t + 3) % RING])
     ring_pass(0, 4)

time: 77.3 us -> 78 us (level)
  no operation moved by 1% of the time
where the time goes in v6:
time: 78 us; the launch traced here: 77.8 us
  Pallas kernels  76.1 us (98%)
  local copies, waits for them, and re-layouts  1.67 us (2%)
    pallas_call x1, Pallas kernels, shards(): pl.pallas_call(body, out_shape=jax.ShapeDtypeStruct((tokens, heads * valu...  76.1 us
    unnamed x1, local copies, waits for them, and re-layouts  1.67 us

profile of v6, /device:TPU:66, one launch (start us, length us, event | category | flops | bytes accessed | tf_op | source)
XLA Modules:
  0.0 77.8 jit_solution(8372692517229692903)
XLA Ops:
  0.0 76.1 %shard_map.55 = bf16[128,1024]{1,0:T(8,128)(2,1)} custom-call(s32[1,16]{1,0:T(1,128)} %lists.1, bf16[16,16,576]{2,1,0:T(8,128)(2,1)} %cache.1, bf16[8,576,128]{2,1,0:T(8,128)(2,1)} %bitcast.1, bf16[8,512,128]{2,1,0:T(8,128)(2,1)} %vup_hbm.1, s32[1024,128]{1,0:T(8,128)} %seg_hbm.1), custom_call_target="tpu_custom_call" | custom-call | tf_op jit(solution)/shard_map/pallas_call | solution.py:373
  76.1 1.7 %copy.7 = bf16[128,1024]{1,0:T(8,128)(2,1)} copy(bf16[128,1024]{1,0:T(8,128)(2,1)} %shard_map.55) | data formatting | bytes 524288
